TPU v7x, 32 devices: a whole 2x2x4 slice. The times are simulated.
32 devices in a mesh: gy: 4 (over y, core), gx: 8 (over z, x).
Axes of the slice: x: 2, y: 2, z: 4, core: 2. Of those that a mesh axis runs over, the one named last changes fastest.
Arguments:
- ocean_blocks: float32 [256, 4, 1024], P('gy', None, 'gx'), may hold values from -4 to 4
- block_map: int32 [256, 8], P('gy', 'gx'), may hold values from 0 to 511, as said below
- velocity: float32 [2, 256, 1024], P(None, 'gy', 'gx'), may hold values from -2 to 2
- stress: float32 [3, 256, 1024], P(None, 'gy', 'gx'), may hold values from -3 to 3
- thickness: float32 [5, 256, 1024], P(None, 'gy', 'gx'), may hold values from 0.05 to 5
- area: float32 [5, 256, 1024], P(None, 'gy', 'gx'), may hold values from 0.1 to 0.2
- wind: float32 [2, 256, 1024], P(None, 'gy', 'gx'), may hold values from -3 to 3
- air_temp: float32 [256, 1024], P('gy', 'gx'), may hold values from -6 to 0
- ice_presence_mask: int32 [256, 1024], P('gy', 'gx'), may hold values 0 or 1
- ocean_land_mask: int32 [256, 1024], P('gy', 'gx'), may hold values 0 or 1
- fold_partner_column: int32 [1024], replicated, may hold values from 0 to 1023, as said below
Outputs:
- velocity_out: float32 [2, 256, 1024], P(None, 'gy', 'gx')
- stress_out: float32 [3, 256, 1024], P(None, 'gy', 'gx')
- thickness_out: float32 [5, 256, 1024], P(None, 'gy', 'gx')
Inputs may be any that keep to these rules, and one draw needn't show every extreme that they name: Within each latitude row of devices block_map is a permutation of 0 to 511; value p * 64 + t names device p, row t. The slots k * 8 to (k + 1) * 8 - 1 of one device all go to one device, into rows k * 8 to (k + 1) * 8 - 1; different k of one device go to different devices. fold_partner_column[i] = (c - i) mod 1024 for one c per draw, so the table is its own inverse.
All inputs are finite; a program needn't handle non-finite values. No bound on the sum of `ice_presence_mask` or of `ocean_land_mask` on one device may be relied on, other than what follows from the above.
Results may differ from a plain program's by a relative error of at most 0.0001.
Values sent between devices are 32-bit elements; how exact they have to be, the bound alone decides.
A program may use at most 64 MiB of HBM per device.

v0:
```python
import jax
import jax.numpy as jnp
from jax import lax
from jax.sharding import PartitionSpec as P

ITERS = 4


RELAX = 0.5
ECC2 = 4.0
DMIN2 = 0.01
PSTAR = 1.0
CSTAR = 5.0
DTE = 0.3
DRAG = 1.0
FCOR = 0.5
KAPPA = 0.5
GAMMA = 0.3
DTT = 0.5
SREF = 34.0


def with_halo(block, sides, width):
    for axis, dim in sides:
        count = lax.axis_size(axis)
        forward = [(i, i + 1) for i in range(count - 1)]
        forward.append((count - 1, 0))
        backward = [(target, source) for source, target in forward]
        low = lax.ppermute(
            lax.slice_in_dim(block, block.shape[dim] - width, None, axis=dim), axis, forward
        )
        high = lax.ppermute(lax.slice_in_dim(block, 0, width, axis=dim), axis, backward)
        block = jnp.concatenate([low, block, high], axis=dim)
    return block


def regroup_local(ocean_blocks, block_map):
    rows, fields, cols = ocean_blocks.shape
    peers = lax.axis_size("gx")
    group = max(2, rows // peers)
    count = rows // group
    target = block_map[:, 0]
    dest_dev = target[::group] // rows
    dest_row = (target % rows).reshape(count, group)
    chosen = dest_dev[None, :] == jnp.arange(peers, dtype=jnp.int32)[:, None]
    blocks = ocean_blocks.reshape(count, group * fields * cols)
    outgoing = jnp.dot(
        chosen.astype(jnp.float32),
        blocks,
        precision=lax.Precision.HIGHEST,
        preferred_element_type=jnp.float32,
    )
    labels = jnp.sum(jnp.where(chosen[:, :, None], dest_row[None, :, :] + 1, 0), axis=1) - 1
    arrived, arrived_rows = (
        lax.all_to_all(outgoing, "gx", split_axis=0, concat_axis=0, tiled=True),
        lax.all_to_all(labels, "gx", split_axis=0, concat_axis=0, tiled=True),
    )
    flat = arrived.reshape(peers * group, fields * cols)
    picks = (
        arrived_rows.reshape(-1)[None, :] == jnp.arange(rows, dtype=jnp.int32)[:, None]
    ).astype(jnp.float32)
    local = jnp.dot(
        picks, flat, precision=lax.Precision.HIGHEST, preferred_element_type=jnp.float32
    )
    return local.reshape(rows, fields, cols)


def attach_rim_halo(field, signs, width, fold_partner_column):
    rows = field.shape[1]
    cols = field.shape[2]
    padded = with_halo(field, (("gy", 1), ("gx", 2)), width)
    top = jnp.flip(field[:, rows - width :, :], axis=1)
    whole_top = lax.all_gather(top, "gx", axis=2, tiled=True)
    total_cols = whole_top.shape[2]
    columns = (
        lax.axis_index("gx") * cols + jnp.arange(-width, cols + width, dtype=jnp.int32)
    ) % total_cols
    north = jnp.take(whole_top, fold_partner_column[columns], axis=2) * signs
    row_pos = lax.axis_index("gy")
    last_row = lax.axis_size("gy") - 1
    upper = jnp.where(row_pos == last_row, north, padded[:, rows + width :, :])
    lower = jnp.where(row_pos == 0, jnp.zeros_like(north), padded[:, :width, :])
    return jnp.concatenate([lower, padded[:, width : rows + width, :], upper], axis=1)


def compute_strain_rates(u_pad, v_pad):
    strain_rate_east = (u_pad[1:-1, 2:] - u_pad[1:-1, :-2]) * 0.5
    strain_rate_north = (v_pad[2:, 1:-1] - v_pad[:-2, 1:-1]) * 0.5
    strain_rate_shear = (
        u_pad[2:, 1:-1] - u_pad[:-2, 1:-1] + (v_pad[1:-1, 2:] - v_pad[1:-1, :-2])
    ) * 0.25
    return (strain_rate_east, strain_rate_north, strain_rate_shear)


def stress_update(old, strain_rate_east, strain_rate_north, strain_rate_shear, strength):
    divergence = strain_rate_east + strain_rate_north
    tension = strain_rate_east - strain_rate_north
    shear = 2.0 * strain_rate_shear
    delta = jnp.sqrt(divergence * divergence + (tension * tension + shear * shear) / ECC2 + DMIN2)
    zeta = strength / delta
    first = (old[0] + RELAX * (zeta * divergence - strength)) / (1.0 + RELAX)
    second = (old[1] + RELAX * zeta * tension / ECC2) / (1.0 + RELAX)
    third = (old[2] + RELAX * zeta * shear / (2.0 * ECC2)) / (1.0 + RELAX)
    return jnp.stack([first, second, third])


def stress_force(padded):
    normal_x = (padded[0] + padded[1]) * 0.5
    normal_y = (padded[0] - padded[1]) * 0.5
    shear = padded[2]
    eastward_force = (normal_x[1:-1, 2:] - normal_x[1:-1, :-2]) * 0.5 + (
        shear[2:, 1:-1] - shear[:-2, 1:-1]
    ) * 0.5
    northward_force = (shear[1:-1, 2:] - shear[1:-1, :-2]) * 0.5 + (
        normal_y[2:, 1:-1] - normal_y[:-2, 1:-1]
    ) * 0.5
    return (eastward_force, northward_force)


def momentum_solve(
    velocity,
    eastward_force,
    northward_force,
    wind,
    ocean_current_east,
    ocean_current_north,
    ice_mass_per_area,
    coriolis_parameter,
    velocity_mask,
):
    east = velocity[0]
    north = velocity[1]
    implicit_denominator = ice_mass_per_area + DTE * DRAG
    right_side_east = east * ice_mass_per_area + DTE * (
        eastward_force
        + wind[0]
        + DRAG * ocean_current_east
        + ice_mass_per_area * coriolis_parameter * north
    )
    right_side_north = north * ice_mass_per_area + DTE * (
        northward_force
        + wind[1]
        + DRAG * ocean_current_north
        - ice_mass_per_area * coriolis_parameter * east
    )
    return jnp.stack(
        [
            velocity_mask * right_side_east / implicit_denominator,
            velocity_mask * right_side_north / implicit_denominator,
        ]
    )


def column_growth(
    thickness,
    velocity,
    ocean_temp,
    ocean_salt,
    ocean_current_east,
    ocean_current_north,
    air_temp,
    omask,
):
    freeze = -0.054 * (SREF + ocean_salt)
    rel_east = velocity[0] - ocean_current_east
    rel_north = velocity[1] - ocean_current_north
    speed = jnp.sqrt(rel_east * rel_east + rel_north * rel_north + 0.01)
    melt = GAMMA * (ocean_temp - freeze) * speed
    growth = KAPPA * (freeze - air_temp) / (thickness + 0.1)
    return omask * jnp.maximum(thickness + DTT * (growth - melt), 0.0)


def body(
    ocean_blocks,
    block_map,
    velocity,
    stress,
    thickness,
    area,
    wind,
    air_temp,
    ice_presence_mask,
    ocean_land_mask,
    fold_partner_column,
):
    ocean = regroup_local(ocean_blocks, block_map)
    ocean_temp = ocean[:, 0, :]
    ocean_salt = ocean[:, 1, :]
    ocean_current_east = ocean[:, 2, :]
    ocean_current_north = ocean[:, 3, :]
    hsum = jnp.sum(area * thickness, axis=0)
    conc = jnp.sum(area, axis=0)
    strength = PSTAR * hsum * jnp.exp(-CSTAR * (1.0 - conc))
    ice_mass_per_area = hsum + 0.2
    rows = velocity.shape[1]
    total_rows = rows * lax.axis_size("gy")
    row_float = (lax.axis_index("gy") * rows + jnp.arange(rows, dtype=jnp.int32)).astype(
        jnp.float32
    )
    coriolis_parameter = (FCOR * (row_float + 0.5) / float(total_rows))[:, None]
    velocity_mask = (ice_presence_mask * ocean_land_mask).astype(jnp.float32)
    omask = ocean_land_mask.astype(jnp.float32)
    velocity_fold_sign = jnp.array([-1.0, -1.0], dtype=jnp.float32).reshape(2, 1, 1)
    ssign = jnp.ones((3, 1, 1), dtype=jnp.float32)
    for step in range(ITERS):
        velocity_padded = attach_rim_halo(velocity, velocity_fold_sign, 1, fold_partner_column)
        strain_rate_east, strain_rate_north, strain_rate_shear = compute_strain_rates(
            velocity_padded[0], velocity_padded[1]
        )
        stress = stress_update(
            stress, strain_rate_east, strain_rate_north, strain_rate_shear, strength
        )
        spad = attach_rim_halo(stress, ssign, 1, fold_partner_column)
        eastward_force, northward_force = stress_force(spad)
        velocity = momentum_solve(
            velocity,
            eastward_force,
            northward_force,
            wind,
            ocean_current_east,
            ocean_current_north,
            ice_mass_per_area,
            coriolis_parameter,
            velocity_mask,
        )
    thickness_out = column_growth(
        thickness,
        velocity,
        ocean_temp,
        ocean_salt,
        ocean_current_east,
        ocean_current_north,
        air_temp,
        omask,
    )
    return (velocity, stress, thickness_out)


def solution(mesh):
    placed = (
        P("gy", None, "gx"),
        P("gy", "gx"),
        P(None, "gy", "gx"),
        P(None, "gy", "gx"),
        P(None, "gy", "gx"),
        P(None, "gy", "gx"),
        P(None, "gy", "gx"),
        P("gy", "gx"),
        P("gy", "gx"),
        P("gy", "gx"),
        P(),
    )
    return jax.shard_map(
        body,
        mesh=mesh,
        in_specs=placed,
        out_specs=(P(None, "gy", "gx"), P(None, "gy", "gx"), P(None, "gy", "gx")),
        check_vma=False,
    )
```

profile of v0, /device:TPU:0, one launch (start us, length us, event | category | flops | bytes accessed | tf_op | source)
XLA Modules:
  0.0 234.9 jit_solution(4450984604818787753)
XLA Ops:
  2.9 7.3 %all-to-all-start = ((s32[8,1,8]{2,1,0:T(1,128)}), s32[8,1,8]{2,1,0:T(1,128)S(1)}, u32[]{:S(2)}, u32[]{:S(2)}) async-start(s32[8,1,8]{2,1,0:T(1,128)} %bitcast.19), calls=%async_computation | async-start | bytes 8192 | tf_op jit(solution)/shard_map/all_to_all | solution.py:56
  13.8 20.8 %all_gather.24 = f32[2,1,1024]{2,1,0:T(1,128)S(1)} all-gather(f32[2,1,128]{2,1,0:T(1,128)S(1)} %get-tuple-element.99), channel_id=1, replica_groups=mesh['gy'=4,'gx'=8] {'gx'}, dimensions={2}, use_global_device_ids=true | all-gather | bytes 9216 | tf_op jit(solution)/shard_map/all_gather | solution.py:73
  34.8 2.0 collective-permute-start.2
  39.3 2.7 %collective-permute-done.2 = f32[2,66,1]{2,1,0:T(8,128)S(1)} collective-permute-done((f32[2,66,1]{2,1,0:T(8,128)S(1)}, f32[2,66,1]{2,1,0:T(8,128)S(1)}, u32[]{:S(2)}, u32[]{:S(2)}) %collective-permute-start.2) | collective-permute-done | bytes 560 | tf_op jit(solution)/shard_map/ppermute | solution.py:29
  44.7 3.4 %all-to-all-start.1 = ((f32[8,1,4096]{2,1,0:T(1,128)}), f32[8,1,4096]{2,1,0:T(1,128)S(1)}, u32[]{:S(2)}, u32[]{:S(2)}) async-start(f32[8,1,4096]{2,1,0:T(1,128)} %copy.72), calls=%async_computation.1 | async-start | bytes 262144 | tf_op jit(solution)/shard_map/all_to_all | solution.py:55
  49.0 4.7 %collective-permute-start.7 = (f32[3,66,1]{2,1,0:T(8,128)S(1)}, f32[3,66,1]{2,1,0:T(8,128)S(1)}, u32[]{:S(2)}, u32[]{:S(2)}) collective-permute-start(f32[3,66,1]{2,1,0:T(8,128)S(1)} %get-tuple-element.76), channel_id=1, source_target_pairs={{1,0},{2,1},{3,2},{4,3},{5,4},{6,5},{7,6},{0,7},{9,8},{10,9},{11,1... | collective-permute-start | bytes 2384 | tf_op jit(solution)/shard_map/ppermute | solution.py:32
  53.7 21.0 %all_gather.25 = f32[3,1,1024]{2,1,0:T(1,128)S(1)} all-gather(f32[3,1,128]{2,1,0:T(1,128)S(1)} %get-tuple-element.83), channel_id=1, replica_groups=mesh['gy'=4,'gx'=8] {'gx'}, dimensions={2}, use_global_device_ids=true | all-gather | bytes 13824 | tf_op jit(solution)/shard_map/all_gather | solution.py:73
  78.9 1.8 collective-permute-done.8
  80.8 2.0 collective-permute-start.10
  82.8 19.0 %all_gather.26 = f32[2,1,1024]{2,1,0:T(1,128)S(1)} all-gather(f32[2,1,128]{2,1,0:T(1,128)S(1)} %get-tuple-element.97), channel_id=1, replica_groups=mesh['gy'=4,'gx'=8] {'gx'}, dimensions={2}, use_global_device_ids=true | all-gather | bytes 9216 | tf_op jit(solution)/shard_map/all_gather | solution.py:73
  104.7 1.8 collective-permute-done.12
  106.7 2.0 collective-permute-start.14
  108.7 19.1 %all_gather.27 = f32[3,1,1024]{2,1,0:T(1,128)S(1)} all-gather(f32[3,1,128]{2,1,0:T(1,128)S(1)} %get-tuple-element.81), channel_id=1, replica_groups=mesh['gy'=4,'gx'=8] {'gx'}, dimensions={2}, use_global_device_ids=true | all-gather | bytes 13824 | tf_op jit(solution)/shard_map/all_gather | solution.py:73
  131.4 1.8 collective-permute-done.16
  133.3 2.0 collective-permute-start.18
  135.3 19.0 %all_gather.28 = f32[2,1,1024]{2,1,0:T(1,128)S(1)} all-gather(f32[2,1,128]{2,1,0:T(1,128)S(1)} %get-tuple-element.95), channel_id=1, replica_groups=mesh['gy'=4,'gx'=8] {'gx'}, dimensions={2}, use_global_device_ids=true | all-gather | bytes 9216 | tf_op jit(solution)/shard_map/all_gather | solution.py:73
  157.2 1.8 collective-permute-done.20
  159.2 2.0 collective-permute-start.22
  161.2 19.1 %all_gather.29 = f32[3,1,1024]{2,1,0:T(1,128)S(1)} all-gather(f32[3,1,128]{2,1,0:T(1,128)S(1)} %get-tuple-element.79), channel_id=1, replica_groups=mesh['gy'=4,'gx'=8] {'gx'}, dimensions={2}, use_global_device_ids=true | all-gather | bytes 13824 | tf_op jit(solution)/shard_map/all_gather | solution.py:73
  185.0 2.0 collective-permute-start.26
  187.0 19.0 %all_gather.30 = f32[2,1,1024]{2,1,0:T(1,128)S(1)} all-gather(f32[2,1,128]{2,1,0:T(1,128)S(1)} %get-tuple-element.93), channel_id=1, replica_groups=mesh['gy'=4,'gx'=8] {'gx'}, dimensions={2}, use_global_device_ids=true | all-gather | bytes 9216 | tf_op jit(solution)/shard_map/all_gather | solution.py:73
  209.0 1.8 collective-permute-done.28
  210.9 2.0 collective-permute-start.30
  212.9 19.1 %all_gather.31 = f32[3,1,1024]{2,1,0:T(1,128)S(1)} all-gather(f32[3,1,128]{2,1,0:T(1,128)S(1)} %get-tuple-element.77), channel_id=1, replica_groups=mesh['gy'=4,'gx'=8] {'gx'}, dimensions={2}, use_global_device_ids=true | all-gather | bytes 13824 | tf_op jit(solution)/shard_map/all_gather | solution.py:73
  (206 shorter events, 36.4 us)
Async XLA Ops:
  2.9 41.9 %all-to-all-start = ((s32[8,1,8]{2,1,0:T(1,128)}), s32[8,1,8]{2,1,0:T(1,128)S(1)}, u32[]{:S(2)}, u32[]{:S(2)}) async-start(s32[8,1,8]{2,1,0:T(1,128)} %bitcast.19), calls=%async_computation | async-start | bytes 8192 | tf_op jit(solution)/shard_map/all_to_all | solution.py:56
  10.9 23.8 %collective-permute-start.1 = (f32[2,1,128]{2,1,0:T(1,128)S(1)}, f32[2,1,128]{2,1,0:T(1,128)S(1)}, u32[]{:S(2)}, u32[]{:S(2)}) collective-permute-start(f32[2,1,128]{2,1,0:T(1,128)S(1)} %get-tuple-element.100), channel_id=1, source_target_pairs={{8,0},{16,8},{24,16},{0,24},{9,1},{17,9},{25,17},{1,25},{10,2},{18... | collective-permute-start | bytes 3080 | tf_op jit(solution)/shard_map/ppermute | solution.py:32
  11.5 23.1 %collective-permute-start = (f32[2,1,128]{2,1,0:T(1,128)S(1)}, f32[2,1,128]{2,1,0:T(1,128)S(1)}, u32[]{:S(2)}, u32[]{:S(2)}) collective-permute-start(f32[2,1,128]{2,1,0:T(1,128)S(1)} %get-tuple-element.99), channel_id=1, source_target_pairs={{0,8},{8,16},{16,24},{24,0},{1,9},{9,17},{17,25},{25,1},{2,10},{10... | collective-permute-start | bytes 3080 | tf_op jit(solution)/shard_map/ppermute | solution.py:29
  34.8 4.5 %collective-permute-start.3 = (f32[2,66,1]{2,1,0:T(8,128)S(1)}, f32[2,66,1]{2,1,0:T(8,128)S(1)}, u32[]{:S(2)}, u32[]{:S(2)}) collective-permute-start(f32[2,66,1]{2,1,0:T(8,128)S(1)} %get-tuple-element.92), channel_id=1, source_target_pairs={{1,0},{2,1},{3,2},{4,3},{5,4},{6,5},{7,6},{0,7},{9,8},{10,9},{11,1... | collective-permute-start | bytes 1592 | tf_op jit(solution)/shard_map/ppermute | solution.py:32
  34.8 7.1 %collective-permute-start.2 = (f32[2,66,1]{2,1,0:T(8,128)S(1)}, f32[2,66,1]{2,1,0:T(8,128)S(1)}, u32[]{:S(2)}, u32[]{:S(2)}) collective-permute-start(f32[2,66,1]{2,1,0:T(8,128)S(1)} %get-tuple-element.91), channel_id=1, source_target_pairs={{0,1},{1,2},{2,3},{3,4},{4,5},{5,6},{6,7},{7,0},{8,9},{9,10},{10,1... | collective-permute-start | bytes 1592 | tf_op jit(solution)/shard_map/ppermute | solution.py:29
  43.4 5.5 %collective-permute-start.5 = (f32[3,1,128]{2,1,0:T(1,128)S(1)}, f32[3,1,128]{2,1,0:T(1,128)S(1)}, u32[]{:S(2)}, u32[]{:S(2)}) collective-permute-start(f32[3,1,128]{2,1,0:T(1,128)S(1)} %get-tuple-element.84), channel_id=1, source_target_pairs={{8,0},{16,8},{24,16},{0,24},{9,1},{17,9},{25,17},{1,25},{10,2},{18... | collective-permute-start | bytes 4616 | tf_op jit(solution)/shard_map/ppermute | solution.py:32
  43.4 5.4 %collective-permute-start.4 = (f32[3,1,128]{2,1,0:T(1,128)S(1)}, f32[3,1,128]{2,1,0:T(1,128)S(1)}, u32[]{:S(2)}, u32[]{:S(2)}) collective-permute-start(f32[3,1,128]{2,1,0:T(1,128)S(1)} %get-tuple-element.83), channel_id=1, source_target_pairs={{0,8},{8,16},{16,24},{24,0},{1,9},{9,17},{17,25},{25,1},{2,10},{10... | collective-permute-start | bytes 4616 | tf_op jit(solution)/shard_map/ppermute | solution.py:29
  44.7 31.3 %all-to-all-start.1 = ((f32[8,1,4096]{2,1,0:T(1,128)}), f32[8,1,4096]{2,1,0:T(1,128)S(1)}, u32[]{:S(2)}, u32[]{:S(2)}) async-start(f32[8,1,4096]{2,1,0:T(1,128)} %copy.72), calls=%async_computation.1 | async-start | bytes 262144 | tf_op jit(solution)/shard_map/all_to_all | solution.py:55
  49.0 26.7 %collective-permute-start.7 = (f32[3,66,1]{2,1,0:T(8,128)S(1)}, f32[3,66,1]{2,1,0:T(8,128)S(1)}, u32[]{:S(2)}, u32[]{:S(2)}) collective-permute-start(f32[3,66,1]{2,1,0:T(8,128)S(1)} %get-tuple-element.76), channel_id=1, source_target_pairs={{1,0},{2,1},{3,2},{4,3},{5,4},{6,5},{7,6},{0,7},{9,8},{10,9},{11,1... | collective-permute-start | bytes 2384 | tf_op jit(solution)/shard_map/ppermute | solution.py:32
  53.7 22.0 %collective-permute-start.6 = (f32[3,66,1]{2,1,0:T(8,128)S(1)}, f32[3,66,1]{2,1,0:T(8,128)S(1)}, u32[]{:S(2)}, u32[]{:S(2)}) collective-permute-start(f32[3,66,1]{2,1,0:T(8,128)S(1)} %get-tuple-element.75), channel_id=1, source_target_pairs={{0,1},{1,2},{2,3},{3,4},{4,5},{5,6},{6,7},{7,0},{8,9},{9,10},{10,1... | collective-permute-start | bytes 2384 | tf_op jit(solution)/shard_map/ppermute | solution.py:29
  80.7 22.1 %collective-permute-start.11 = (f32[2,66,1]{2,1,0:T(8,128)S(1)}, f32[2,66,1]{2,1,0:T(8,128)S(1)}, u32[]{:S(2)}, u32[]{:S(2)}) collective-permute-start(f32[2,66,1]{2,1,0:T(8,128)S(1)} %get-tuple-element.90), channel_id=1, source_target_pairs={{1,0},{2,1},{3,2},{4,3},{5,4},{6,5},{7,6},{0,7},{9,8},{10,9},{11,1... | collective-permute-start | bytes 1592 | tf_op jit(solution)/shard_map/ppermute | solution.py:32
  80.8 22.0 %collective-permute-start.10 = (f32[2,66,1]{2,1,0:T(8,128)S(1)}, f32[2,66,1]{2,1,0:T(8,128)S(1)}, u32[]{:S(2)}, u32[]{:S(2)}) collective-permute-start(f32[2,66,1]{2,1,0:T(8,128)S(1)} %get-tuple-element.89), channel_id=1, source_target_pairs={{0,1},{1,2},{2,3},{3,4},{4,5},{5,6},{6,7},{7,0},{8,9},{9,10},{10,1... | collective-permute-start | bytes 1592 | tf_op jit(solution)/shard_map/ppermute | solution.py:29
  103.5 3.1 %collective-permute-start.12 = (f32[3,1,128]{2,1,0:T(1,128)S(1)}, f32[3,1,128]{2,1,0:T(1,128)S(1)}, u32[]{:S(2)}, u32[]{:S(2)}) collective-permute-start(f32[3,1,128]{2,1,0:T(1,128)S(1)} %get-tuple-element.81), channel_id=1, source_target_pairs={{0,8},{8,16},{16,24},{24,0},{1,9},{9,17},{17,25},{25,1},{2,10},{10... | collective-permute-start | bytes 4616 | tf_op jit(solution)/shard_map/ppermute | solution.py:29
  106.6 22.1 %collective-permute-start.15 = (f32[3,66,1]{2,1,0:T(8,128)S(1)}, f32[3,66,1]{2,1,0:T(8,128)S(1)}, u32[]{:S(2)}, u32[]{:S(2)}) collective-permute-start(f32[3,66,1]{2,1,0:T(8,128)S(1)} %get-tuple-element.74), channel_id=1, source_target_pairs={{1,0},{2,1},{3,2},{4,3},{5,4},{6,5},{7,6},{0,7},{9,8},{10,9},{11,1... | collective-permute-start | bytes 2384 | tf_op jit(solution)/shard_map/ppermute | solution.py:32
  106.7 22.0 %collective-permute-start.14 = (f32[3,66,1]{2,1,0:T(8,128)S(1)}, f32[3,66,1]{2,1,0:T(8,128)S(1)}, u32[]{:S(2)}, u32[]{:S(2)}) collective-permute-start(f32[3,66,1]{2,1,0:T(8,128)S(1)} %get-tuple-element.73), channel_id=1, source_target_pairs={{0,1},{1,2},{2,3},{3,4},{4,5},{5,6},{6,7},{7,0},{8,9},{9,10},{10,1... | collective-permute-start | bytes 2384 | tf_op jit(solution)/shard_map/ppermute | solution.py:29
  133.2 22.1 %collective-permute-start.19 = (f32[2,66,1]{2,1,0:T(8,128)S(1)}, f32[2,66,1]{2,1,0:T(8,128)S(1)}, u32[]{:S(2)}, u32[]{:S(2)}) collective-permute-start(f32[2,66,1]{2,1,0:T(8,128)S(1)} %get-tuple-element.88), channel_id=1, source_target_pairs={{1,0},{2,1},{3,2},{4,3},{5,4},{6,5},{7,6},{0,7},{9,8},{10,9},{11,1... | collective-permute-start | bytes 1592 | tf_op jit(solution)/shard_map/ppermute | solution.py:32
  133.3 22.0 %collective-permute-start.18 = (f32[2,66,1]{2,1,0:T(8,128)S(1)}, f32[2,66,1]{2,1,0:T(8,128)S(1)}, u32[]{:S(2)}, u32[]{:S(2)}) collective-permute-start(f32[2,66,1]{2,1,0:T(8,128)S(1)} %get-tuple-element.87), channel_id=1, source_target_pairs={{0,1},{1,2},{2,3},{3,4},{4,5},{5,6},{6,7},{7,0},{8,9},{9,10},{10,1... | collective-permute-start | bytes 1592 | tf_op jit(solution)/shard_map/ppermute | solution.py:29
  155.9 3.1 %collective-permute-start.20 = (f32[3,1,128]{2,1,0:T(1,128)S(1)}, f32[3,1,128]{2,1,0:T(1,128)S(1)}, u32[]{:S(2)}, u32[]{:S(2)}) collective-permute-start(f32[3,1,128]{2,1,0:T(1,128)S(1)} %get-tuple-element.79), channel_id=1, source_target_pairs={{0,8},{8,16},{16,24},{24,0},{1,9},{9,17},{17,25},{25,1},{2,10},{10... | collective-permute-start | bytes 4616 | tf_op jit(solution)/shard_map/ppermute | solution.py:29
  159.1 22.1 %collective-permute-start.23 = (f32[3,66,1]{2,1,0:T(8,128)S(1)}, f32[3,66,1]{2,1,0:T(8,128)S(1)}, u32[]{:S(2)}, u32[]{:S(2)}) collective-permute-start(f32[3,66,1]{2,1,0:T(8,128)S(1)} %get-tuple-element.72), channel_id=1, source_target_pairs={{1,0},{2,1},{3,2},{4,3},{5,4},{6,5},{7,6},{0,7},{9,8},{10,9},{11,1... | collective-permute-start | bytes 2384 | tf_op jit(solution)/shard_map/ppermute | solution.py:32
  159.2 22.0 %collective-permute-start.22 = (f32[3,66,1]{2,1,0:T(8,128)S(1)}, f32[3,66,1]{2,1,0:T(8,128)S(1)}, u32[]{:S(2)}, u32[]{:S(2)}) collective-permute-start(f32[3,66,1]{2,1,0:T(8,128)S(1)} %get-tuple-element.71), channel_id=1, source_target_pairs={{0,1},{1,2},{2,3},{3,4},{4,5},{5,6},{6,7},{7,0},{8,9},{9,10},{10,1... | collective-permute-start | bytes 2384 | tf_op jit(solution)/shard_map/ppermute | solution.py:29
  184.9 22.1 %collective-permute-start.27 = (f32[2,66,1]{2,1,0:T(8,128)S(1)}, f32[2,66,1]{2,1,0:T(8,128)S(1)}, u32[]{:S(2)}, u32[]{:S(2)}) collective-permute-start(f32[2,66,1]{2,1,0:T(8,128)S(1)} %get-tuple-element.86), channel_id=1, source_target_pairs={{1,0},{2,1},{3,2},{4,3},{5,4},{6,5},{7,6},{0,7},{9,8},{10,9},{11,1... | collective-permute-start | bytes 1592 | tf_op jit(solution)/shard_map/ppermute | solution.py:32
  185.0 22.0 %collective-permute-start.26 = (f32[2,66,1]{2,1,0:T(8,128)S(1)}, f32[2,66,1]{2,1,0:T(8,128)S(1)}, u32[]{:S(2)}, u32[]{:S(2)}) collective-permute-start(f32[2,66,1]{2,1,0:T(8,128)S(1)} %get-tuple-element.85), channel_id=1, source_target_pairs={{0,1},{1,2},{2,3},{3,4},{4,5},{5,6},{6,7},{7,0},{8,9},{9,10},{10,1... | collective-permute-start | bytes 1592 | tf_op jit(solution)/shard_map/ppermute | solution.py:29
  210.9 22.1 %collective-permute-start.31 = (f32[3,66,1]{2,1,0:T(8,128)S(1)}, f32[3,66,1]{2,1,0:T(8,128)S(1)}, u32[]{:S(2)}, u32[]{:S(2)}) collective-permute-start(f32[3,66,1]{2,1,0:T(8,128)S(1)} %get-tuple-element.70), channel_id=1, source_target_pairs={{1,0},{2,1},{3,2},{4,3},{5,4},{6,5},{7,6},{0,7},{9,8},{10,9},{11,1... | collective-permute-start | bytes 2384 | tf_op jit(solution)/shard_map/ppermute | solution.py:32
  210.9 22.0 %collective-permute-start.30 = (f32[3,66,1]{2,1,0:T(8,128)S(1)}, f32[3,66,1]{2,1,0:T(8,128)S(1)}, u32[]{:S(2)}, u32[]{:S(2)}) collective-permute-start(f32[3,66,1]{2,1,0:T(8,128)S(1)} %get-tuple-element.69), channel_id=1, source_target_pairs={{0,1},{1,2},{2,3},{3,4},{4,5},{5,6},{6,7},{7,0},{8,9},{9,10},{10,1... | collective-permute-start | bytes 2384 | tf_op jit(solution)/shard_map/ppermute | solution.py:29
  (22 other events, 63.2 us)
where the time goes:
time: 235 us
  blocking collectives  156 us (66%)
  starting transfers between devices  34.4 us (15%)
  waiting for transfers between devices  19.5 us (8%)
  local copies, waits for them, and re-layouts  15.1 us (6%)
  other arithmetic  7.87 us (3%)
    all_gather x8, blocking collectives, attach_rim_halo(): whole_top = lax.all_gather(top, 'gx', axis=2, tiled=True)  156 us
    ppermute x16, starting transfers between devices, with_halo(): lax.ppermute(lax.slice_in_dim(block, block.shape[dim] - width, None, axis...  17.6 us
    ppermute x16, waiting for transfers between devices, with_halo(): lax.ppermute(lax.slice_in_dim(block, block.shape[dim] - width, None, axis...  13.2 us
    all_to_all x1, starting transfers between devices, regroup_local(): lax.all_to_all(labels, 'gx', split_axis=0, concat_axis=0, tiled=True)  7.25 us
    gather x17, local copies, waits for them, and re-layouts, attach_rim_halo(): north = jnp.take(whole_top, fold_partner_column[columns], axis=2) * signs  7.09 us
    ppermute x16, waiting for transfers between devices, with_halo(): lax.ppermute(lax.slice_in_dim(block, 0, width, axis=dim), axis, backward)  6.25 us
    ppermute x16, starting transfers between devices, with_halo(): lax.ppermute(lax.slice_in_dim(block, 0, width, axis=dim), axis, backward)  6.19 us
  transfers between devices with their start and end apart: 34, of which 14 were waited for; matrix products, arithmetic and copies ran while one was open for 5% of the time, Pallas kernels for 0%

commit v1 on v0

v1 whole, which is shorter than its diff:
```python
import functools

import jax
import jax.numpy as jnp
from jax import lax
from jax.experimental import pallas as pl
from jax.experimental.pallas import tpu as pltpu
from jax.sharding import PartitionSpec as P

ITERS = 4
HALO = 8
MESH = pl.DeviceIdType.MESH
F32 = jnp.float32
DIRS = ((0, 1), (0, -1), (1, 0), (1, 1), (1, -1), (-1, 0), (-1, 1), (-1, -1))


def exact_dot(a, b, contract):
    return lax.dot_general(
        a,
        b,
        ((contract, (0,)), ((), ())),
        precision=lax.Precision.HIGHEST,
        preferred_element_type=F32,
    )


def each(count, fn):
    if count <= 8:
        for i in range(1, count):
            fn(i)
    else:
        lax.fori_loop(1, count, lambda i, c: (fn(i), c)[1], 0)


def flip8(x):
    row = lax.broadcasted_iota(jnp.int32, x.shape, 0)
    x = pltpu.roll(x, 4, axis=0)
    x = jnp.where((row // 2) % 2 == 0, pltpu.roll(x, 6, axis=0), pltpu.roll(x, 2, axis=0))
    return jnp.where(row % 2 == 0, pltpu.roll(x, 7, axis=0), pltpu.roll(x, 1, axis=0))


def pack(tiles):
    lane = lax.broadcasted_iota(jnp.int32, tiles[0].shape, 1) // 16
    out = pltpu.roll(tiles[0], 8, axis=1)
    for t in range(1, len(tiles)):
        out = jnp.where(lane == t, pltpu.roll(tiles[t], (8 + 16 * t) % 128, axis=1), out)
    return out


def unpack(west, east, count):
    lane = lax.broadcasted_iota(jnp.int32, west.shape, 1) % 16
    both = jnp.where(lane < 8, west, east)
    return [pltpu.roll(both, (120 - 16 * t) % 128, axis=1) for t in range(count)]


def kernel(
    n,
    m,
    ocean_ref,
    map_ref,
    vel_ref,
    str_ref,
    thick_ref,
    area_ref,
    wind_ref,
    air_ref,
    ice_ref,
    land_ref,
    fold_ref,
    vel_out,
    str_out,
    thick_out,
    ext,
    lext,
    a2a_out,
    a2a_in,
    ex_out,
    ex_in,
    ey_out,
    ey_in,
    ec_out,
    ec_in,
    lx_out,
    lx_in,
    ly_out,
    ly_in,
    lc_out,
    lc_in,
    efold_out,
    efold,
    lfold_out,
    lfold,
    a2a_ss,
    a2a_rs,
    e_ss,
    e_rs,
    l_ss,
    l_rs,
    ef_ss,
    ef_rs,
    lf_ss,
    lf_rs,
):
    rows, cols = air_ref.shape
    group = a2a_out.shape[2]
    gy = lax.axis_index("gy")
    gx = lax.axis_index("gx")
    last = m - 1
    top = gy == last
    has_n = gy < last
    has_s = gy > 0
    barrier = pltpu.get_barrier_semaphore()

    def gxi(off):
        return lax.rem(gx + off + n, n)

    def greet(off):
        pl.semaphore_signal(barrier, inc=1, device_id=(gy, gxi(off)), device_id_type=MESH)

    each(n, greet)
    for dy, cond in ((1, has_n), (-1, has_s)):

        @pl.when(cond)
        def _():
            for dx in (-1, 0, 1):
                pl.semaphore_signal(
                    barrier, inc=1, device_id=(gy + dy, gxi(dx)), device_id_type=MESH
                )

    target = map_ref[...]
    pos = (target // rows) * group + lax.rem(target, group)
    lanes = -(-(n * group) // 128) * 128
    sel_t = (pos == lax.broadcasted_iota(jnp.int32, (rows, lanes), 1)).astype(F32)
    slot_group = lax.broadcasted_iota(jnp.int32, (rows, cols), 0) // group + 1
    fields = [ocean_ref[:, f, :] for f in range(4)] + [slot_group.astype(F32)]
    for f in range(5):
        sorted_f = exact_dot(sel_t, fields[f], (0,))
        for p in range(n):
            a2a_out[p, f] = sorted_f[p * group : (p + 1) * group, :]

    count = (n - 1) + jnp.where(has_n, 3, 0) + jnp.where(has_s, 3, 0)
    pl.semaphore_wait(barrier, count)

    def a2a(off):
        return pltpu.make_async_remote_copy(
            src_ref=a2a_out.at[gxi(off)],
            dst_ref=a2a_in.at[off],
            send_sem=a2a_ss.at[off],
            recv_sem=a2a_rs.at[off],
            device_id=(gy, gxi(off)),
            device_id_type=MESH,
        )

    each(n, lambda off: a2a(off).start())

    area = [area_ref[c] for c in range(area_ref.shape[0])]
    thick = [thick_ref[c] for c in range(area_ref.shape[0])]
    hsum = area[0] * thick[0]
    conc = area[0]
    for c in range(1, len(area)):
        hsum = hsum + area[c] * thick[c]
        conc = conc + area[c]
    strength = hsum * jnp.exp(-5.0 * (1.0 - conc))
    mass = hsum + 0.2
    vmask = (ice_ref[...] * land_ref[...]).astype(F32)
    coef = vmask / (mass + 0.3)
    early = [
        vel_ref[0],
        vel_ref[1],
        str_ref[0],
        str_ref[1],
        str_ref[2],
        strength,
        coef * mass,
        coef * 0.3,
    ]
    esigns = (-1.0, -1.0, 1.0, 1.0, 1.0, 1.0, 1.0, 1.0)
    lsigns = (-1.0, -1.0)

    def prepare(vals, signs, e, x_out, y_out, c_out, fold_out, fold):
        tiles = rows // 8
        for f, val in enumerate(vals):
            e[f, HALO : HALO + rows, cols:] = val
            x_out[f] = pack([val[8 * t : 8 * t + 8] for t in range(tiles)])
            y_out[0, f] = val[rows - 8 :]
            y_out[1, f] = val[:8]
        c_out[0] = pack([val[rows - 8 :] for val in vals])
        c_out[1] = pack([val[:8] for val in vals])

        @pl.when(top)
        def _():
            for f in range(len(vals)):
                mirrored = flip8(y_out[0, f]) * signs[f]
                fold_out[f] = mirrored
                fold[0, f] = mirrored

    def halo(d, x_out, x_in, y_out, y_in, c_out, c_in, ss, rs):
        dy, dx = DIRS[d]
        if dy == 0:
            src, dst = x_out, x_in.at[0 if dx == 1 else 1]
        elif dx == 0:
            which = 0 if dy == 1 else 1
            src, dst = y_out.at[which], y_in.at[which]
        else:
            which = 0 if dy == 1 else 1
            src, dst = c_out.at[which], c_in.at[which, 0 if dx == 1 else 1]
        return pltpu.make_async_remote_copy(
            src_ref=src,
            dst_ref=dst,
            send_sem=ss.at[d],
            recv_sem=rs.at[d],
            device_id=(gy + dy, gxi(dx)),
            device_id_type=MESH,
        )

    def folding(off, fold_out, fold, ss, rs):
        return pltpu.make_async_remote_copy(
            src_ref=fold_out,
            dst_ref=fold.at[off],
            send_sem=ss.at[off],
            recv_sem=rs.at[off],
            device_id=(gy, gxi(off)),
            device_id_type=MESH,
        )

    def start(hargs, fargs):
        @pl.when(top)
        def _():
            each(n, lambda off: folding(off, *fargs).start())

        for d in (0, 1):
            halo(d, *hargs).start()

        @pl.when(has_n)
        def _():
            for d in (2, 3, 4):
                halo(d, *hargs).start()

        @pl.when(has_s)
        def _():
            for d in (5, 6, 7):
                halo(d, *hargs).start()

    def wait_sends(hargs, fargs):
        @pl.when(top)
        def _():
            each(n, lambda off: folding(off, *fargs).wait_send())

        for d in (0, 1):
            halo(d, *hargs).wait_send()

        @pl.when(has_n)
        def _():
            for d in (2, 3, 4):
                halo(d, *hargs).wait_send()

        @pl.when(has_s)
        def _():
            for d in (5, 6, 7):
                halo(d, *hargs).wait_send()

    def receive(nf, e, hargs, fargs):
        _, x_in, _, y_in, _, c_in, _, _ = hargs
        _, fold, _, _ = fargs
        for d in (0, 1):
            halo(d, *hargs).wait_recv()
        for f in range(nf):
            for t, tile in enumerate(unpack(x_in[0, f], x_in[1, f], rows // 8)):
                e[f, HALO + 8 * t : HALO + 8 * t + 8, :cols] = tile

        @pl.when(has_s)
        def _():
            for d in (2, 3, 4):
                halo(d, *hargs).wait_recv()
            corner = unpack(c_in[0, 0], c_in[0, 1], nf)
            for f in range(nf):
                e[f, :HALO, cols:] = y_in[0, f]
                e[f, :HALO, :cols] = corner[f]

        @pl.when(gy == 0)
        def _():
            for f in range(nf):
                e[f, :HALO, :] = jnp.zeros((HALO, 2 * cols), F32)

        @pl.when(has_n)
        def _():
            for d in (5, 6, 7):
                halo(d, *hargs).wait_recv()
            corner = unpack(c_in[1, 0], c_in[1, 1], nf)
            for f in range(nf):
                e[f, HALO + rows :, cols:] = y_in[1, f]
                e[f, HALO + rows :, :cols] = corner[f]

        @pl.when(top)
        def _():
            each(n, lambda off: folding(off, *fargs).wait_recv())
            total = n * cols
            c = fold_ref[0]
            base = c - (gx + 1) * cols - 8 + 2 * total
            first = base // cols
            lane = lax.broadcasted_iota(jnp.int32, (3 * cols, 2 * cols), 1)
            kk = lax.broadcasted_iota(jnp.int32, (3 * cols, 2 * cols), 0)
            column = gx * cols + lane - cols + jnp.where(lane < cols // 2, 2 * cols, 0)
            rel = c + 2 * total - column - first * cols
            picks = (kk == rel).astype(F32)
            blocks = []
            for b in range(3):
                slot = lax.rem(gx + 4 * n - first - b, n)
                blocks.append(fold[slot].reshape(nf * 8, cols))
            north = exact_dot(jnp.concatenate(blocks, axis=1), picks, (1,))
            for f in range(nf):
                e[f, HALO + rows :, :] = north[8 * f : 8 * f + 8, :]

    eargs = (ex_out, ex_in, ey_out, ey_in, ec_out, ec_in, e_ss, e_rs)
    efargs = (efold_out, efold, ef_ss, ef_rs)
    largs = (lx_out, lx_in, ly_out, ly_in, lc_out, lc_in, l_ss, l_rs)
    lfargs = (lfold_out, lfold, lf_ss, lf_rs)
    prepare(early, esigns, ext, ex_out, ey_out, ec_out, efold_out, efold)
    start(eargs, efargs)

    a2a_in[0] = a2a_out[gx]
    row_group = lax.broadcasted_iota(jnp.int32, (rows, cols), 0) // group + 1
    row_group = row_group.astype(F32)

    def place(i, acc):
        label = jnp.concatenate([a2a_in[i, 4]] * (rows // group), axis=0)
        hit = label == row_group
        return tuple(
            jnp.where(hit, jnp.concatenate([a2a_in[i, f]] * (rows // group), axis=0), acc[f])
            for f in range(4)
        )

    acc = tuple(jnp.zeros((rows, cols), F32) for _ in range(4))
    each(n, lambda off: a2a(off).wait_recv())
    if n <= 8:
        for i in range(n):
            acc = place(i, acc)
    else:
        acc = lax.fori_loop(0, n, place, acc)
    temp, salt, east, north = acc
    late = [wind_ref[0] + east, wind_ref[1] + north]
    prepare(late, lsigns, lext, lx_out, ly_out, lc_out, lfold_out, lfold)
    start(largs, lfargs)

    freeze = -0.054 * (34.0 + salt)
    excess = 0.15 * (temp - freeze)
    gap = 0.25 * (freeze - air_ref[...])
    for c in range(thick_ref.shape[0]):
        h = thick_ref[c]
        thick_out[c] = h + gap / (h + 0.1)

    receive(8, ext, eargs, efargs)
    u, v, s1, s2, s3, strn, ca, cb = [ext[f] for f in range(8)]
    wide = (rows + 2 * HALO, 2 * cols)
    g1 = g2 = cc = None
    for step in range(ITERS):
        ue = pltpu.roll(u, wide[1] - 1, axis=1) - pltpu.roll(u, 1, axis=1)
        vn = pltpu.roll(v, wide[0] - 1, axis=0) - pltpu.roll(v, 1, axis=0)
        un = pltpu.roll(u, wide[0] - 1, axis=0) - pltpu.roll(u, 1, axis=0)
        ve = pltpu.roll(v, wide[1] - 1, axis=1) - pltpu.roll(v, 1, axis=1)
        div = (ue + vn) * 0.5
        ten = (ue - vn) * 0.5
        she = (un + ve) * 0.5
        zeta = strn * lax.rsqrt(div * div + (ten * ten + she * she) * 0.25 + 0.01)
        s1 = s1 * (2.0 / 3.0) + (zeta * div - strn) * (1.0 / 3.0)
        s2 = s2 * (2.0 / 3.0) + zeta * ten * (1.0 / 12.0)
        s3 = s3 * (2.0 / 3.0) + zeta * she * (1.0 / 24.0)
        if step == 0:
            receive(2, lext, largs, lfargs)
            g1, g2 = lext[0], lext[1]
            grow = gy * rows - HALO + lax.broadcasted_iota(jnp.int32, wide, 0)
            grow = jnp.where(grow >= m * rows, 2 * m * rows - 1 - grow, grow)
            cc = ca * ((0.3 * 0.5 / (m * rows)) * (grow.astype(F32) + 0.5))
        sx = s1 + s2
        sy = s1 - s2
        fx = (pltpu.roll(sx, wide[1] - 1, axis=1) - pltpu.roll(sx, 1, axis=1)) * 0.25 + (
            pltpu.roll(s3, wide[0] - 1, axis=0) - pltpu.roll(s3, 1, axis=0)
        ) * 0.5
        fy = (pltpu.roll(s3, wide[1] - 1, axis=1) - pltpu.roll(s3, 1, axis=1)) * 0.5 + (
            pltpu.roll(sy, wide[0] - 1, axis=0) - pltpu.roll(sy, 1, axis=0)
        ) * 0.25
        u, v = ca * u + cc * v + cb * (fx + g1), ca * v - cc * u + cb * (fy + g2)

    inner = slice(HALO, HALO + rows)
    vel_out[0] = u[inner, cols:]
    vel_out[1] = v[inner, cols:]
    str_out[0] = s1[inner, cols:]
    str_out[1] = s2[inner, cols:]
    str_out[2] = s3[inner, cols:]
    de = u[inner, cols:] - east
    dn = v[inner, cols:] - north
    melt = excess * jnp.sqrt(de * de + dn * dn + 0.01)
    land = land_ref[...].astype(F32)
    for c in range(thick_ref.shape[0]):
        thick_out[c] = land * jnp.maximum(thick_out[c] - melt, 0.0)

    each(n, lambda off: a2a(off).wait_send())
    wait_sends(eargs, efargs)
    wait_sends(largs, lfargs)


def body(n, m, *args):
    ocean, block_map, vel, stress, thick = args[:5]
    rows, cols = args[7].shape
    group = max(2, rows // n)
    nf, nl = 8, 2
    wide = (rows + 2 * HALO, 2 * cols)
    vmem = pl.BlockSpec(memory_space=pltpu.VMEM)
    smem = pl.BlockSpec(memory_space=pltpu.SMEM)

    def bufs(k):
        return [
            pltpu.VMEM((k, 8, cols), F32),
            pltpu.VMEM((2, k, 8, cols), F32),
            pltpu.VMEM((2, k, 8, cols), F32),
            pltpu.VMEM((2, k, 8, cols), F32),
            pltpu.VMEM((2, 8, cols), F32),
            pltpu.VMEM((2, 2, 8, cols), F32),
        ]

    dma = pltpu.SemaphoreType.DMA
    return pl.pallas_call(
        functools.partial(kernel, n, m),
        out_shape=(
            jax.ShapeDtypeStruct(vel.shape, F32),
            jax.ShapeDtypeStruct(stress.shape, F32),
            jax.ShapeDtypeStruct(thick.shape, F32),
        ),
        in_specs=[vmem] * 10 + [smem],
        out_specs=(vmem, vmem, vmem),
        scratch_shapes=[
            pltpu.VMEM((nf,) + wide, F32),
            pltpu.VMEM((nl,) + wide, F32),
            pltpu.VMEM((n, 5, group, cols), F32),
            pltpu.VMEM((n, 5, group, cols), F32),
            *bufs(nf),
            *bufs(nl),
            pltpu.VMEM((nf, 8, cols), F32),
            pltpu.VMEM((n, nf, 8, cols), F32),
            pltpu.VMEM((nl, 8, cols), F32),
            pltpu.VMEM((n, nl, 8, cols), F32),
            dma((n,)),
            dma((n,)),
            dma((8,)),
            dma((8,)),
            dma((8,)),
            dma((8,)),
            dma((n,)),
            dma((n,)),
            dma((n,)),
            dma((n,)),
        ],
        compiler_params=pltpu.CompilerParams(
            collective_id=0, has_side_effects=True, vmem_limit_bytes=24 * 1024 * 1024
        ),
    )(*args)


def solution(mesh):
    placed = (
        P("gy", None, "gx"),
        P("gy", "gx"),
        P(None, "gy", "gx"),
        P(None, "gy", "gx"),
        P(None, "gy", "gx"),
        P(None, "gy", "gx"),
        P(None, "gy", "gx"),
        P("gy", "gx"),
        P("gy", "gx"),
        P("gy", "gx"),
        P(),
    )
    return jax.shard_map(
        functools.partial(body, mesh.shape["gx"], mesh.shape["gy"]),
        mesh=mesh,
        in_specs=placed,
        out_specs=(P(None, "gy", "gx"), P(None, "gy", "gx"), P(None, "gy", "gx")),
        check_vma=False,
    )
```

time: 235 us -> 31.2 us (0.13)
  the two profiles are of different devices: /device:TPU:0 before, /device:TPU:1 now
where the time goes in v1:
time: 31.2 us; the launch traced here: 30.7 us
  Pallas kernels  19.8 us (63%)
  local copies, waits for them, and re-layouts  10.2 us (33%)
  between operations  0.66 us (2%)
    pallas_call x1, Pallas kernels, body(): pl.pallas_call(functools.partial(kernel, n, m), out_shape=(jax.ShapeDtype...  19.8 us
    unnamed x24, local copies, waits for them, and re-layouts  10.2 us

profile of v1, /device:TPU:1, one launch (start us, length us, event | category | flops | bytes accessed | tf_op | source)
XLA Modules:
  0.0 30.7 jit_solution(15568028398593343682)
XLA Ops:
  0.6 0.0 copy-start.6
  0.6 0.8 %copy.14.map_ref = s32[64,1]{1,0:T(8,128)S(1)} copy(s32[64,1]{0,1:T(1,128)} %param.12) | data formatting | bytes 512 | tf_op args[1]
  1.4 0.0 copy-done.6
  1.4 0.0 copy-start
  1.4 0.9 %copy-done = f32[5,64,128]{2,1,0:T(8,128)S(1)} copy-done((f32[5,64,128]{2,1,0:T(8,128)S(1)}, f32[5,64,128]{2,1,0:T(8,128)}, u32[]{:S(2)}) %copy-start) | copy-done | bytes 163864
  2.3 0.0 copy-start.1
  2.3 0.9 %copy-done.1 = f32[5,64,128]{2,1,0:T(8,128)S(1)} copy-done((f32[5,64,128]{2,1,0:T(8,128)S(1)}, f32[5,64,128]{2,1,0:T(8,128)}, u32[]{:S(2)}) %copy-start.1) | copy-done | bytes 163864
  3.2 0.0 copy-start.2
  3.2 0.9 %copy-done.2 = f32[64,4,128]{2,1,0:T(4,128)S(1)} copy-done((f32[64,4,128]{2,1,0:T(4,128)S(1)}, f32[64,4,128]{2,1,0:T(4,128)}, u32[]{:S(2)}) %copy-start.2) | copy-done | bytes 131096
  4.1 0.0 copy-start.3
  4.1 0.9 %copy-done.3 = f32[3,64,128]{2,1,0:T(8,128)S(1)} copy-done((f32[3,64,128]{2,1,0:T(8,128)S(1)}, f32[3,64,128]{2,1,0:T(8,128)}, u32[]{:S(2)}) %copy-start.3) | copy-done | bytes 98328
  5.0 0.0 copy-start.4
  5.0 0.8 %copy-done.4 = f32[2,64,128]{2,1,0:T(8,128)S(1)} copy-done((f32[2,64,128]{2,1,0:T(8,128)S(1)}, f32[2,64,128]{2,1,0:T(8,128)}, u32[]{:S(2)}) %copy-start.4) | copy-done | bytes 65560
  5.9 0.0 copy-start.5
  5.9 0.8 %copy-done.5 = f32[2,64,128]{2,1,0:T(8,128)S(1)} copy-done((f32[2,64,128]{2,1,0:T(8,128)S(1)}, f32[2,64,128]{2,1,0:T(8,128)}, u32[]{:S(2)}) %copy-start.5) | copy-done | bytes 65560
  6.7 0.0 copy-start.7
  6.7 0.8 %copy-done.7 = s32[64,128]{1,0:T(8,128)S(1)} copy-done((s32[64,128]{1,0:T(8,128)S(1)}, s32[64,128]{1,0:T(8,128)}, u32[]{:S(2)}) %copy-start.7) | copy-done | bytes 32792
  7.5 0.0 copy-start.8
  7.5 0.8 %copy-done.8 = s32[64,128]{1,0:T(8,128)S(1)} copy-done((s32[64,128]{1,0:T(8,128)S(1)}, s32[64,128]{1,0:T(8,128)}, u32[]{:S(2)}) %copy-start.8) | copy-done | bytes 32792
  8.2 0.7 %copy-done.9 = s32[1024]{0:T(1024)S(1)} copy-done((s32[1024]{0:T(1024)S(1)}, s32[1024]{0:T(1024)}, u32[]{:S(2)}) %copy-start.9) | copy-done | bytes 4120
  8.9 19.8 %shard_map.130 = (f32[2,64,128]{2,1,0:T(8,128)S(1)}, f32[3,64,128]{2,1,0:T(8,128)S(1)}, f32[5,64,128]{2,1,0:T(8,128)S(1)}) custom-call(f32[64,4,128]{2,1,0:T(4,128)S(1)} %copy-done.2, s32[64,1]{1,0:T(8,128)S(1)} %copy.14.map_ref, f32[2,64,128]{2,1,0:T(8,128)S(1)} %copy-done.4, f32[3,64,128]{2,1,0:T(8,128)S(1)} %copy-done.3, f32[5,64,128]{2,1,0:T(8,128)S(1)} %copy-done, ...), custom_call_target="tpu_custom_call" | custom-call | tf_op jit(solution)/shard_map/pallas_call | solution.py:422
  28.7 0.6 %copy.18 = f32[2,64,128]{2,1,0:T(8,128)} copy(f32[2,64,128]{2,1,0:T(8,128)S(1)} %get-tuple-element.6) | data formatting | bytes 131072
  29.4 0.6 %copy.19 = f32[3,64,128]{2,1,0:T(8,128)} copy(f32[3,64,128]{2,1,0:T(8,128)S(1)} %get-tuple-element.7) | data formatting | bytes 196608
  30.0 0.7 %copy.20 = f32[5,64,128]{2,1,0:T(8,128)} copy(f32[5,64,128]{2,1,0:T(8,128)S(1)} %get-tuple-element.8) | data formatting | bytes 327680
  (1 shorter events, 0.0 us)
Async XLA Ops:
  0.6 0.8 %copy-start.6 = (f32[64,128]{1,0:T(8,128)S(1)}, f32[64,128]{1,0:T(8,128)}, u32[]{:S(2)}) copy-start(f32[64,128]{1,0:T(8,128)} %air_ref.1) | copy-start | bytes 98308
  1.4 0.9 %copy-start = (f32[5,64,128]{2,1,0:T(8,128)S(1)}, f32[5,64,128]{2,1,0:T(8,128)}, u32[]{:S(2)}) copy-start(f32[5,64,128]{2,1,0:T(8,128)} %thick_ref.1) | copy-start | bytes 491524
  2.3 0.9 %copy-start.1 = (f32[5,64,128]{2,1,0:T(8,128)S(1)}, f32[5,64,128]{2,1,0:T(8,128)}, u32[]{:S(2)}) copy-start(f32[5,64,128]{2,1,0:T(8,128)} %area_ref.1) | copy-start | bytes 491524
  3.2 0.9 %copy-start.2 = (f32[64,4,128]{2,1,0:T(4,128)S(1)}, f32[64,4,128]{2,1,0:T(4,128)}, u32[]{:S(2)}) copy-start(f32[64,4,128]{2,1,0:T(4,128)} %ocean_ref.1) | copy-start | bytes 393220
  4.1 0.9 %copy-start.3 = (f32[3,64,128]{2,1,0:T(8,128)S(1)}, f32[3,64,128]{2,1,0:T(8,128)}, u32[]{:S(2)}) copy-start(f32[3,64,128]{2,1,0:T(8,128)} %str_ref.1) | copy-start | bytes 294916
  5.0 0.8 %copy-start.4 = (f32[2,64,128]{2,1,0:T(8,128)S(1)}, f32[2,64,128]{2,1,0:T(8,128)}, u32[]{:S(2)}) copy-start(f32[2,64,128]{2,1,0:T(8,128)} %vel_ref.1) | copy-start | bytes 196612
  5.9 0.8 %copy-start.5 = (f32[2,64,128]{2,1,0:T(8,128)S(1)}, f32[2,64,128]{2,1,0:T(8,128)}, u32[]{:S(2)}) copy-start(f32[2,64,128]{2,1,0:T(8,128)} %wind_ref.1) | copy-start | bytes 196612
  6.7 0.8 %copy-start.7 = (s32[64,128]{1,0:T(8,128)S(1)}, s32[64,128]{1,0:T(8,128)}, u32[]{:S(2)}) copy-start(s32[64,128]{1,0:T(8,128)} %ice_ref.1) | copy-start | bytes 98308
  7.5 0.8 %copy-start.8 = (s32[64,128]{1,0:T(8,128)S(1)}, s32[64,128]{1,0:T(8,128)}, u32[]{:S(2)}) copy-start(s32[64,128]{1,0:T(8,128)} %land_ref.1) | copy-start | bytes 98308
  8.2 0.7 %copy-start.9 = (s32[1024]{0:T(1024)S(1)}, s32[1024]{0:T(1024)}, u32[]{:S(2)}) copy-start(s32[1024]{0:T(1024)} %fold_ref.1) | copy-start | bytes 12292

commit v2 on v1

--- a/solution.py
+++ b/solution.py
@@ -14,14 +14,16 @@
 DIRS = ((0, 1), (0, -1), (1, 0), (1, 1), (1, -1), (-1, 0), (-1, 1), (-1, -1))
 
 
-def exact_dot(a, b, contract):
-    return lax.dot_general(
-        a,
-        b,
-        ((contract, (0,)), ((), ())),
-        precision=lax.Precision.HIGHEST,
-        preferred_element_type=F32,
-    )
+def pieces(x):
+    high = x.astype(jnp.bfloat16)
+    rest = x - high.astype(F32)
+    middle = rest.astype(jnp.bfloat16)
+    low = (rest - middle.astype(F32)).astype(jnp.bfloat16)
+    return high, middle, low
+
+
+def dot(a, b):
+    return jnp.dot(a, b, preferred_element_type=F32)
 
 
 def each(count, fn):
@@ -56,6 +58,20 @@
 def kernel(
     n,
     m,
+    ocean_hbm,
+    map_hbm,
+    vel_hbm,
+    str_hbm,
+    thick_hbm,
+    area_hbm,
+    wind_hbm,
+    air_hbm,
+    ice_hbm,
+    land_hbm,
+    fold_hbm,
+    vel_out,
+    str_out,
+    thick_out,
     ocean_ref,
     map_ref,
     vel_ref,
@@ -67,9 +83,7 @@
     ice_ref,
     land_ref,
     fold_ref,
-    vel_out,
-    str_out,
-    thick_out,
+    in_sem,
     ext,
     lext,
     a2a_out,
@@ -127,14 +141,37 @@
                     barrier, inc=1, device_id=(gy + dy, gxi(dx)), device_id_type=MESH
                 )
 
+    pairs = (
+        (ocean_hbm, ocean_ref),
+        (map_hbm, map_ref),
+        (area_hbm, area_ref),
+        (thick_hbm, thick_ref),
+        (vel_hbm, vel_ref),
+        (str_hbm, str_ref),
+        (ice_hbm, ice_ref),
+        (land_hbm, land_ref),
+        (wind_hbm, wind_ref),
+        (air_hbm, air_ref),
+        (fold_hbm, fold_ref),
+    )
+    loads = [pltpu.make_async_copy(src, dst, in_sem.at[i]) for i, (src, dst) in enumerate(pairs)]
+    for load in loads:
+        load.start()
+    loads[0].wait()
+    loads[1].wait()
+
     target = map_ref[...]
     pos = (target // rows) * group + lax.rem(target, group)
-    lanes = -(-(n * group) // 128) * 128
-    sel_t = (pos == lax.broadcasted_iota(jnp.int32, (rows, lanes), 1)).astype(F32)
+    order = lax.broadcasted_iota(jnp.int32, (n * group, rows), 0)
+    picked = (jnp.broadcast_to(pos, (n * group, rows)) == order).astype(jnp.bfloat16)
     slot_group = lax.broadcasted_iota(jnp.int32, (rows, cols), 0) // group + 1
     fields = [ocean_ref[:, f, :] for f in range(4)] + [slot_group.astype(F32)]
     for f in range(5):
-        sorted_f = exact_dot(sel_t, fields[f], (0,))
+        if f < 4:
+            high, middle, low = pieces(fields[f])
+            sorted_f = (dot(picked, high) + dot(picked, middle)) + dot(picked, low)
+        else:
+            sorted_f = dot(picked, fields[f].astype(jnp.bfloat16))
         for p in range(n):
             a2a_out[p, f] = sorted_f[p * group : (p + 1) * group, :]
 
@@ -152,6 +189,8 @@
         )
 
     each(n, lambda off: a2a(off).start())
+    for load in loads[2:]:
+        load.wait()
 
     area = [area_ref[c] for c in range(area_ref.shape[0])]
     thick = [thick_ref[c] for c in range(area_ref.shape[0])]
@@ -302,12 +341,13 @@
             kk = lax.broadcasted_iota(jnp.int32, (3 * cols, 2 * cols), 0)
             column = gx * cols + lane - cols + jnp.where(lane < cols // 2, 2 * cols, 0)
             rel = c + 2 * total - column - first * cols
-            picks = (kk == rel).astype(F32)
+            picks = (kk == rel).astype(jnp.bfloat16)
             blocks = []
             for b in range(3):
                 slot = lax.rem(gx + 4 * n - first - b, n)
                 blocks.append(fold[slot].reshape(nf * 8, cols))
-            north = exact_dot(jnp.concatenate(blocks, axis=1), picks, (1,))
+            high, middle, low = pieces(jnp.concatenate(blocks, axis=1))
+            north = (dot(high, picks) + dot(middle, picks)) + dot(low, picks)
             for f in range(nf):
                 e[f, HALO + rows :, :] = north[8 * f : 8 * f + 8, :]
 
@@ -406,7 +446,8 @@
     nf, nl = 8, 2
     wide = (rows + 2 * HALO, 2 * cols)
     vmem = pl.BlockSpec(memory_space=pltpu.VMEM)
-    smem = pl.BlockSpec(memory_space=pltpu.SMEM)
+    hbm = pl.BlockSpec(memory_space=pltpu.MemorySpace.HBM)
+    args = tuple(pltpu.with_memory_space_constraint(a, pltpu.MemorySpace.HBM) for a in (ocean, block_map.T) + args[2:])
 
     def bufs(k):
         return [
@@ -426,9 +467,12 @@
             jax.ShapeDtypeStruct(stress.shape, F32),
             jax.ShapeDtypeStruct(thick.shape, F32),
         ),
-        in_specs=[vmem] * 10 + [smem],
+        in_specs=[hbm] * 11,
         out_specs=(vmem, vmem, vmem),
         scratch_shapes=[
+            *[pltpu.VMEM(a.shape, a.dtype) for a in args[:10]],
+            pltpu.SMEM(args[10].shape, jnp.int32),
+            dma((11,)),
             pltpu.VMEM((nf,) + wide, F32),
             pltpu.VMEM((nl,) + wide, F32),
             pltpu.VMEM((n, 5, group, cols), F32),

time: 31.2 us -> 22.1 us (0.71); the launches traced: 30.7 us -> 21.9 us
  local copies, waits for them, and re-layouts: 10.2 us -> 1.94 us
  Pallas kernels: 19.8 us -> 19.3 us
    unnamed x24 -> x3, local copies, waits for them, and re-layouts: 10.2 us -> 1.94 us
    pallas_call x1, Pallas kernels: 19.8 us -> 19.3 us  [body(): pl.pallas_call(functools.partial(kernel, n, m), out_shape=(jax.ShapeDtype...]
where the time goes in v2:
time: 22.1 us; the launch traced here: 21.9 us
  Pallas kernels  19.3 us (87%)
  local copies, waits for them, and re-layouts  1.94 us (9%)
  between operations  0.64 us (3%)
    pallas_call x1, Pallas kernels, body(): pl.pallas_call(functools.partial(kernel, n, m), out_shape=(jax.ShapeDtype...  19.3 us
    unnamed x3, local copies, waits for them, and re-layouts  1.94 us

profile of v2, /device:TPU:1, one launch (start us, length us, event | category | flops | bytes accessed | tf_op | source)
XLA Modules:
  0.0 21.9 jit_solution(14033950922643478375)
XLA Ops:
  0.6 19.3 %shard_map.130 = (f32[2,64,128]{2,1,0:T(8,128)S(1)}, f32[3,64,128]{2,1,0:T(8,128)S(1)}, f32[5,64,128]{2,1,0:T(8,128)S(1)}) custom-call(f32[64,4,128]{2,1,0:T(4,128)} %ocean_hbm.1, s32[1,64]{1,0:T(1,128)} %bitcast.1, f32[2,64,128]{2,1,0:T(8,128)} %vel_hbm.1, f32[3,64,128]{2,1,0:T(8,128)} %str_hbm.1, f32[5,64,128]{2,1,0:T(8,128)} %thick_hbm.1, ...), custom_call_target="tpu_custom_call" | custom-call | tf_op jit(solution)/shard_map/pallas_call | solution.py:463
  20.0 0.6 %copy.17 = f32[2,64,128]{2,1,0:T(8,128)} copy(f32[2,64,128]{2,1,0:T(8,128)S(1)} %get-tuple-element.6) | data formatting | bytes 131072
  20.6 0.6 %copy.18 = f32[3,64,128]{2,1,0:T(8,128)} copy(f32[3,64,128]{2,1,0:T(8,128)S(1)} %get-tuple-element.7) | data formatting | bytes 196608
  21.3 0.7 %copy.19 = f32[5,64,128]{2,1,0:T(8,128)} copy(f32[5,64,128]{2,1,0:T(8,128)S(1)} %get-tuple-element.8) | data formatting | bytes 327680

commit v3 on v2

--- a/solution.py
+++ b/solution.py
@@ -84,6 +84,7 @@
     land_ref,
     fold_ref,
     in_sem,
+    picks_ref,
     ext,
     lext,
     a2a_out,
@@ -298,6 +299,9 @@
             for d in (5, 6, 7):
                 halo(d, *hargs).wait_send()
 
+    def first_block():
+        return (fold_ref[0] - (gx + 1) * cols - 8 + 2 * n * cols) // cols
+
     def receive(nf, e, hargs, fargs):
         _, x_in, _, y_in, _, c_in, _, _ = hargs
         _, fold, _, _ = fargs
@@ -333,15 +337,8 @@
         @pl.when(top)
         def _():
             each(n, lambda off: folding(off, *fargs).wait_recv())
-            total = n * cols
-            c = fold_ref[0]
-            base = c - (gx + 1) * cols - 8 + 2 * total
-            first = base // cols
-            lane = lax.broadcasted_iota(jnp.int32, (3 * cols, 2 * cols), 1)
-            kk = lax.broadcasted_iota(jnp.int32, (3 * cols, 2 * cols), 0)
-            column = gx * cols + lane - cols + jnp.where(lane < cols // 2, 2 * cols, 0)
-            rel = c + 2 * total - column - first * cols
-            picks = (kk == rel).astype(jnp.bfloat16)
+            first = first_block()
+            picks = picks_ref[...]
             blocks = []
             for b in range(3):
                 slot = lax.rem(gx + 4 * n - first - b, n)
@@ -351,12 +348,23 @@
             for f in range(nf):
                 e[f, HALO + rows :, :] = north[8 * f : 8 * f + 8, :]
 
+    def build_picks():
+        @pl.when(top)
+        def _():
+            first = first_block()
+            lane = lax.broadcasted_iota(jnp.int32, (3 * cols, 2 * cols), 1)
+            kk = lax.broadcasted_iota(jnp.int32, (3 * cols, 2 * cols), 0)
+            column = gx * cols + lane - cols + jnp.where(lane < cols // 2, 2 * cols, 0)
+            rel = fold_ref[0] + 2 * n * cols - column - first * cols
+            picks_ref[...] = (kk == rel).astype(jnp.bfloat16)
+
     eargs = (ex_out, ex_in, ey_out, ey_in, ec_out, ec_in, e_ss, e_rs)
     efargs = (efold_out, efold, ef_ss, ef_rs)
     largs = (lx_out, lx_in, ly_out, ly_in, lc_out, lc_in, l_ss, l_rs)
     lfargs = (lfold_out, lfold, lf_ss, lf_rs)
     prepare(early, esigns, ext, ex_out, ey_out, ec_out, efold_out, efold)
     start(eargs, efargs)
+    build_picks()
 
     a2a_in[0] = a2a_out[gx]
     row_group = lax.broadcasted_iota(jnp.int32, (rows, cols), 0) // group + 1
@@ -392,6 +400,7 @@
     receive(8, ext, eargs, efargs)
     u, v, s1, s2, s3, strn, ca, cb = [ext[f] for f in range(8)]
     wide = (rows + 2 * HALO, 2 * cols)
+    inner = slice(HALO, HALO + rows)
     g1 = g2 = cc = None
     for step in range(ITERS):
         ue = pltpu.roll(u, wide[1] - 1, axis=1) - pltpu.roll(u, 1, axis=1)
@@ -411,24 +420,26 @@
             grow = gy * rows - HALO + lax.broadcasted_iota(jnp.int32, wide, 0)
             grow = jnp.where(grow >= m * rows, 2 * m * rows - 1 - grow, grow)
             cc = ca * ((0.3 * 0.5 / (m * rows)) * (grow.astype(F32) + 0.5))
-        sx = s1 + s2
-        sy = s1 - s2
-        fx = (pltpu.roll(sx, wide[1] - 1, axis=1) - pltpu.roll(sx, 1, axis=1)) * 0.25 + (
-            pltpu.roll(s3, wide[0] - 1, axis=0) - pltpu.roll(s3, 1, axis=0)
-        ) * 0.5
-        fy = (pltpu.roll(s3, wide[1] - 1, axis=1) - pltpu.roll(s3, 1, axis=1)) * 0.5 + (
-            pltpu.roll(sy, wide[0] - 1, axis=0) - pltpu.roll(sy, 1, axis=0)
-        ) * 0.25
-        u, v = ca * u + cc * v + cb * (fx + g1), ca * v - cc * u + cb * (fy + g2)
-
-    inner = slice(HALO, HALO + rows)
-    vel_out[0] = u[inner, cols:]
-    vel_out[1] = v[inner, cols:]
+        part = (lambda x: x[inner, cols:]) if step == ITERS - 1 else (lambda x: x)
+
+        def along(x):
+            return part(pltpu.roll(x, wide[1] - 1, axis=1)) - part(pltpu.roll(x, 1, axis=1))
+
+        def across(x):
+            return part(pltpu.roll(x, wide[0] - 1, axis=0)) - part(pltpu.roll(x, 1, axis=0))
+
+        fx = along(s1 + s2) * 0.25 + across(s3) * 0.5
+        fy = along(s3) * 0.5 + across(s1 - s2) * 0.25
+        u, v, a, b, c = part(u), part(v), part(ca), part(cb), part(cc)
+        u, v = a * u + c * v + b * (fx + part(g1)), a * v - c * u + b * (fy + part(g2))
+
+    vel_out[0] = u
+    vel_out[1] = v
     str_out[0] = s1[inner, cols:]
     str_out[1] = s2[inner, cols:]
     str_out[2] = s3[inner, cols:]
-    de = u[inner, cols:] - east
-    dn = v[inner, cols:] - north
+    de = u - east
+    dn = v - north
     melt = excess * jnp.sqrt(de * de + dn * dn + 0.01)
     land = land_ref[...].astype(F32)
     for c in range(thick_ref.shape[0]):
@@ -437,6 +448,15 @@
     each(n, lambda off: a2a(off).wait_send())
     wait_sends(eargs, efargs)
     wait_sends(largs, lfargs)
+
+
+def emit(vel, stress, thick, vel_out, str_out, thick_out, sem):
+    pairs = ((vel, vel_out), (stress, str_out), (thick, thick_out))
+    copies = [pltpu.make_async_copy(src, dst, sem.at[i]) for i, (src, dst) in enumerate(pairs)]
+    for copy in copies:
+        copy.start()
+    for copy in copies:
+        copy.wait()
 
 
 def body(n, m, *args):
@@ -460,19 +480,21 @@
         ]
 
     dma = pltpu.SemaphoreType.DMA
-    return pl.pallas_call(
+    shapes = (
+        jax.ShapeDtypeStruct(vel.shape, F32),
+        jax.ShapeDtypeStruct(stress.shape, F32),
+        jax.ShapeDtypeStruct(thick.shape, F32),
+    )
+    results = pl.pallas_call(
         functools.partial(kernel, n, m),
-        out_shape=(
-            jax.ShapeDtypeStruct(vel.shape, F32),
-            jax.ShapeDtypeStruct(stress.shape, F32),
-            jax.ShapeDtypeStruct(thick.shape, F32),
-        ),
+        out_shape=shapes,
         in_specs=[hbm] * 11,
         out_specs=(vmem, vmem, vmem),
         scratch_shapes=[
             *[pltpu.VMEM(a.shape, a.dtype) for a in args[:10]],
             pltpu.SMEM(args[10].shape, jnp.int32),
             dma((11,)),
+            pltpu.VMEM((3 * cols, 2 * cols), jnp.bfloat16),
             pltpu.VMEM((nf,) + wide, F32),
             pltpu.VMEM((nl,) + wide, F32),
             pltpu.VMEM((n, 5, group, cols), F32),
@@ -498,6 +520,14 @@
             collective_id=0, has_side_effects=True, vmem_limit_bytes=24 * 1024 * 1024
         ),
     )(*args)
+    return pl.pallas_call(
+        emit,
+        out_shape=shapes,
+        in_specs=[vmem] * 3,
+        out_specs=(hbm, hbm, hbm),
+        scratch_shapes=[dma((3,))],
+        compiler_params=pltpu.CompilerParams(vmem_limit_bytes=1024 * 1024),
+    )(*results)
 
 
 def solution(mesh):

time: 22.1 us -> 20.8 us (0.941)
  local copies, waits for them, and re-layouts: 1.94 us -> 0 us
  Pallas kernels: 19.3 us -> 20 us
    unnamed x3 -> x0, local copies, waits for them, and re-layouts: 1.94 us -> none
    pallas_call x1 -> x2, Pallas kernels: 19.3 us -> 20 us  [the longest x1 19.3 us: body(): pl.pallas_call(functools.partial(kernel, n, m), out_shape=shapes, in_spec...]
where the time goes in v3:
time: 20.8 us; the launch traced here: 20.7 us
  Pallas kernels  20 us (96%)
  between operations  0.64 us (3%)
    pallas_call x1, Pallas kernels, body(): pl.pallas_call(functools.partial(kernel, n, m), out_shape=shapes, in_spec...  19.3 us
    pallas_call x1, Pallas kernels, body(): pl.pallas_call(emit, out_shape=shapes, in_specs=[vmem] * 3, out_specs=(hb...  0.75 us

profile of v3, /device:TPU:1, one launch (start us, length us, event | category | flops | bytes accessed | tf_op | source)
XLA Modules:
  0.0 20.7 jit_solution(2930209851059628482)
XLA Ops:
  0.6 19.3 %shard_map.130 = (f32[2,64,128]{2,1,0:T(8,128)S(1)}, f32[3,64,128]{2,1,0:T(8,128)S(1)}, f32[5,64,128]{2,1,0:T(8,128)S(1)}) custom-call(f32[64,4,128]{2,1,0:T(4,128)} %ocean_hbm.1, s32[1,64]{1,0:T(1,128)} %bitcast.1, f32[2,64,128]{2,1,0:T(8,128)} %vel_hbm.1, f32[3,64,128]{2,1,0:T(8,128)} %str_hbm.1, f32[5,64,128]{2,1,0:T(8,128)} %thick_hbm.1, ...), custom_call_target="tpu_custom_call" | custom-call | tf_op jit(solution)/shard_map/pallas_call | solution.py:488
  19.9 0.7 %shard_map.131 = (f32[2,64,128]{2,1,0:T(8,128)}, f32[3,64,128]{2,1,0:T(8,128)}, f32[5,64,128]{2,1,0:T(8,128)}) custom-call(f32[2,64,128]{2,1,0:T(8,128)S(1)} %get-tuple-element.6.vel, f32[3,64,128]{2,1,0:T(8,128)S(1)} %get-tuple-element.7.stress, f32[5,64,128]{2,1,0:T(8,128)S(1)} %get-tuple-element.8.thick), custom_call_target="tpu_custom_call" | custom-call | tf_op jit(solution)/shard_map/pallas_call | solution.py:523
